TPU v7x, 32 devices: a whole 2x2x4 slice. The times are simulated.
32 devices in a mesh: group: 2 (over x), expert: 8 (over z, y), tensor: 2 (over core).
Axes of the slice: x: 2, y: 2, z: 4, core: 2. Of those that a mesh axis runs over, the one named last changes fastest.
Arguments:
- tokens: bfloat16 [2048, 4096], P(('group', 'expert'), 'tensor'), parts along dimension 0, may hold values from -6 to 6
- latent_down: bfloat16 [4096, 1024], P('tensor'), may hold values from -0.09375 to 0.09375
- expert_gate: bfloat16 [8, 1024, 2048], P('expert', None, 'tensor'), may hold values from -0.1875 to 0.1875
- expert_up: bfloat16 [8, 1024, 2048], P('expert', None, 'tensor'), may hold values from -0.1875 to 0.1875
- expert_down: bfloat16 [8, 2048, 1024], P('expert', 'tensor'), may hold values from -0.125 to 0.125
- routes: int32 [2048, 4], P(('group', 'expert')), parts along dimension 0, may hold values from 0 to 7, all different within a row; in each aligned block of 128 rows (0 to 127, 128 to 255, ...) at most 128 rows name the same one
- gates: float32 [2048, 4], P(('group', 'expert')), parts along dimension 0, may hold values from 0.1 to 1
Outputs:
- mixed: bfloat16 [2048, 1024], P(('group', 'expert'), 'tensor'), parts along dimension 0
There are 2 independent parts, one for each index of `group`. A program takes and returns all parts, laid end to end along the dimension named above; an argument that names none is the same for every part. Nothing has to cross between parts.
Inputs may be any that keep to these rules, and one draw needn't show every extreme that they name: `routes`: the 4 experts of a row differ. The rows of one aligned block of 128 name one expert at most 128 times, and in every draw some block names some expert exactly 128 times.
All inputs are finite; a program needn't handle non-finite values.
Results may differ from a plain program's by a relative error of at most 0.0071.
Values may be sent and summed in bfloat16 or wider, within the bound.
A program may use at most 64 MiB of HBM per device.

v0:
```python
import jax
import jax.numpy as jnp
from jax import lax
from jax.sharding import PartitionSpec as P


def slot_tables(route_rows, gate_rows, devices, capacity):
    row_count, per_row = route_rows.shape
    pick_ids = route_rows.reshape(-1)
    expert_ids = jnp.arange(devices, dtype=jnp.int32)
    onehot = (pick_ids[:, None] == expert_ids[None, :]).astype(jnp.int32)
    earlier = jnp.cumsum(onehot, axis=0) - onehot
    position = jnp.sum(earlier * onehot, axis=1)
    slot_ids = pick_ids * capacity + position
    all_slots = jnp.arange(devices * capacity, dtype=jnp.int32)
    slot_hits = (slot_ids[None, :] == all_slots[:, None]).astype(jnp.float32)
    slot_hits = slot_hits.reshape(devices * capacity, row_count, per_row)
    placing = jnp.sum(slot_hits, axis=2).astype(jnp.bfloat16)
    mixing = jnp.sum(slot_hits * gate_rows[None, :, :], axis=2).T
    return (placing, mixing)


def on_device(tokens, latent_down, expert_gate, expert_up, expert_down, routes, gates):
    devices = lax.axis_size("expert")
    row_count, per_row = routes.shape
    capacity = 2 * row_count * per_row // devices
    placing, mixing = slot_tables(routes, gates, devices, capacity)
    partial_latent = jnp.dot(tokens, latent_down, preferred_element_type=jnp.float32)
    w_gate = expert_gate[0]
    w_up = expert_up[0]
    w_down = expert_down[0]
    latent = lax.psum_scatter(partial_latent, "tensor", scatter_dimension=1, tiled=True).astype(
        jnp.bfloat16
    )
    outgoing = jnp.dot(placing, latent, preferred_element_type=jnp.float32).astype(jnp.bfloat16)
    outgoing = outgoing.reshape(devices, capacity, latent.shape[1])
    slot_rows = lax.all_gather(
        lax.all_to_all(outgoing, "expert", split_axis=0, concat_axis=0, tiled=True),
        "tensor",
        axis=2,
        tiled=True,
    )
    gate_part = jnp.einsum("snl,lh->snh", slot_rows, w_gate, preferred_element_type=jnp.float32)
    up_part = jnp.einsum("snl,lh->snh", slot_rows, w_up, preferred_element_type=jnp.float32)
    hidden = (jax.nn.silu(gate_part) * up_part).astype(jnp.bfloat16)
    partial_value = jnp.einsum("snh,hl->snl", hidden, w_down, preferred_element_type=jnp.float32)
    results = lax.psum_scatter(partial_value, "tensor", scatter_dimension=2, tiled=True).astype(
        jnp.bfloat16
    )
    returned = lax.all_to_all(results, "expert", split_axis=0, concat_axis=0, tiled=True)
    returned_rows = returned.reshape(devices * capacity, returned.shape[2]).astype(jnp.float32)
    mixed = jnp.dot(
        mixing, returned_rows, precision=lax.Precision.HIGHEST, preferred_element_type=jnp.float32
    )
    return mixed.astype(jnp.bfloat16)


def solution(mesh):
    return jax.shard_map(
        on_device,
        mesh=mesh,
        in_specs=(
            P(("group", "expert"), "tensor"),
            P("tensor", None),
            P("expert", None, "tensor"),
            P("expert", None, "tensor"),
            P("expert", "tensor", None),
            P(("group", "expert"), None),
            P(("group", "expert"), None),
        ),
        out_specs=P(("group", "expert"), "tensor"),
        check_vma=False,
    )
```

profile of v0, /device:TPU:0, one launch (start us, length us, event | category | flops | bytes accessed | tf_op | source)
XLA Modules:
  0.0 135.6 jit_solution(16325493301194705626)
XLA Ops:
  6.5 0.0 copy-start
  6.5 0.0 copy-start.1
  6.5 0.0 copy-start.2
  6.5 0.0 reduce-scatter.3.cloned.1.call-start
  6.5 4.0 %fusion.13 = f32[128,1024]{1,0:T(8,128)} fusion(bf16[128,2048]{1,0:T(8,128)(2,1)} %param.7, bf16[2048,1024]{1,0:T(8,128)(2,1)} %param.8), kind=kOutput, calls=%fused_computation.22 | convolution fusion | flops 536870912 | bytes 5242880 | tf_op jit(solution)/shard_map/dot_general | solution.py:28
  10.5 0.0 reduce-scatter.3.cloned.1.call-update
  10.6 0.0 all-gather.2.cloned.1.call-start
  10.6 0.0 copy-done.1
  10.6 0.1 copy.20
  10.7 0.1 eq.43
  10.8 0.1 eq.39
  11.0 1.1 reduce-window.6
  12.1 0.2 slice_reduce_fusion
  12.4 0.1 fusion.10
  12.5 0.1 reduce_sum.30
  12.6 0.1 copy.22
  12.7 0.0 copy-done.2
  12.7 0.5 convert_reduce_fusion
  13.1 8.2 %reduce-scatter.3.cloned.1.call-done = f32[128,512]{1,0:T(8,128)} async-done(((f32[128,1024]{1,0:T(8,128)}), f32[128,512]{1,0:T(8,128)}) %reduce-scatter.3.cloned.1.call-update) | async-done | bytes 262160 | tf_op jit(solution)/shard_map/reduce_scatter | solution.py:32
  21.4 1.4 %convolution_convert_fusion = bf16[1024,512]{1,0:T(8,128)(2,1)S(1)} fusion(bf16[1024,128]{1,0:T(8,128)(2,1)S(1)} %get-tuple-element.5, f32[128,512]{1,0:T(8,128)} %reduce-scatter.3.cloned.1.call-done), kind=kOutput, calls=%fused_computation.9 | convolution fusion | flops 134807552 | bytes 1572864 | tf_op jit(solution)/shard_map/dot_general | solution.py:35
  22.7 31.9 %all_to_all.10 = bf16[8,128,512]{2,1,0:T(8,128)(2,1)} all-to-all(bf16[8,128,512]{2,1,0:T(8,128)(2,1)S(1)} %bitcast.31), channel_id=1, replica_groups=mesh['group'=2,'expert'=8,'tensor'=2] {'expert'}, dimensions={0} | all-to-all | bytes 2097152 | tf_op jit(solution)/shard_map/all_to_all | solution.py:38
  54.6 0.0 all-gather.2.cloned.1.call-update
  54.6 0.0 reduce-scatter.5.cloned.1.call-start
  54.7 9.7 %all-gather.2.cloned.1.call-done = bf16[8,128,1024]{2,1,0:T(8,128)(2,1)} async-done(((bf16[8,128,512]{2,1,0:T(8,128)(2,1)}), bf16[8,128,1024]{2,1,0:T(8,128)(2,1)}) %all-gather.2.cloned.1.call-update) | async-done | bytes 2097168 | tf_op jit(solution)/shard_map/all_gather | solution.py:37
  64.4 0.0 copy-done
  64.4 5.9 %fusion.3 = f32[8,128,1024]{2,1,0:T(8,128)} fusion(bf16[8,128,1024]{2,1,0:T(8,128)(2,1)} %all-gather.2.cloned.1.call-done, bf16[1,1024,1024]{2,1,0:T(8,128)(2,1)S(1)} %copy-done), kind=kOutput, calls=%fused_computation.4 | convolution fusion | flops 2147483648 | bytes 8388608 | tf_op jit(solution)/shard_map/snl,lh->snh/dot_general | solution.py:43
  70.3 10.5 %fusion = f32[8,128,1024]{2,1,0:T(8,128)} fusion(bf16[1,1024,1024]{2,1,0:T(8,128)(2,1)} %param.11, f32[8,128,1024]{2,1,0:T(8,128)} %fusion.3, bf16[8,128,1024]{2,1,0:T(8,128)(2,1)} %all-gather.2.cloned.1.call-done, bf16[1,1024,1024]{2,1,0:T(8,128)(2,1)} %param.10), kind=kOutput, calls=%fused_computation.1 | convolution fusion | flops 4301258752 | bytes 14680064 | tf_op jit(solution)/shard_map/snh,hl->snl/dot_general | solution.py:46
  80.8 0.0 reduce-scatter.5.cloned.1.call-update
  80.8 13.4 %reduce-scatter.5.cloned.1.call-done = f32[8,128,512]{2,1,0:T(8,128)} async-done(((f32[8,128,1024]{2,1,0:T(8,128)}), f32[8,128,512]{2,1,0:T(8,128)}) %reduce-scatter.5.cloned.1.call-update) | async-done | bytes 2097168 | tf_op jit(solution)/shard_map/reduce_scatter | solution.py:47
  94.2 1.7 %convert_element_type.37 = bf16[8,128,512]{2,1,0:T(8,128)(2,1)S(1)} convert(f32[8,128,512]{2,1,0:T(8,128)} %reduce-scatter.5.cloned.1.call-done) | non-fusion elementwise | flops 524288 | bytes 3145728 | tf_op jit(solution)/shard_map/convert_element_type | solution.py:47
  95.9 31.8 %all_to_all.11 = bf16[8,128,512]{2,1,0:T(8,128)(2,1)S(1)} all-to-all(bf16[8,128,512]{2,1,0:T(8,128)(2,1)S(1)} %convert_element_type.37), channel_id=1, replica_groups=mesh['group'=2,'expert'=8,'tensor'=2] {'expert'}, dimensions={0} | all-to-all | bytes 2097152 | tf_op jit(solution)/shard_map/all_to_all | solution.py:50
  127.7 1.4 %convolution_convert_fusion.1 = bf16[128,512]{1,0:T(8,128)(2,1)} fusion(f32[1024,128]{1,0:T(8,128)S(1)} %get-tuple-element.6, bf16[1024,512]{1,0:T(8,128)(2,1)S(1)} %bitcast.32), kind=kOutput, calls=%fused_computation.10 | convolution fusion | flops 805371904 | bytes 1703936 | tf_op jit(solution)/shard_map/dot_general | solution.py:52
  (4 shorter events, 0.1 us)
Async XLA Ops:
  6.5 57.9 %copy-start = (bf16[1,1024,1024]{2,1,0:T(8,128)(2,1)S(1)}, bf16[1,1024,1024]{2,1,0:T(8,128)(2,1)}, u32[]{:S(2)}) copy-start(bf16[1,1024,1024]{2,1,0:T(8,128)(2,1)} %param.9) | copy-start | bytes 6291460
  6.5 4.1 %copy-start.1 = (s32[128,4]{0,1:T(4,128)S(1)}, s32[128,4]{0,1:T(4,128)}, u32[]{:S(2)}) copy-start(s32[128,4]{0,1:T(4,128)} %param.12) | copy-start | bytes 6148
  6.5 6.1 %copy-start.2 = (f32[128,4]{0,1:T(4,128)S(1)}, f32[128,4]{0,1:T(4,128)}, u32[]{:S(2)}) copy-start(f32[128,4]{0,1:T(4,128)} %param.13) | copy-start | bytes 6148
  6.5 14.8 %reduce-scatter.3.cloned.1.call-start = ((), (), s32[]{:S(2)}) async-start(), calls=%async_computation.4 | async-start | bytes 786432 | tf_op jit(solution)/shard_map/reduce_scatter | solution.py:32
  10.6 53.8 %all-gather.2.cloned.1.call-start = ((), (), s32[]{:S(2)}) async-start(), calls=%async_computation.5 | async-start | bytes 3145728 | tf_op jit(solution)/shard_map/all_gather | solution.py:37
  54.6 39.6 %reduce-scatter.5.cloned.1.call-start = ((), (), s32[]{:S(2)}) async-start(), calls=%async_computation.6 | async-start | bytes 6291456 | tf_op jit(solution)/shard_map/reduce_scatter | solution.py:47
Sparse Core Ops, SparseCore 0:
  10.7 10.6 reduce-scatter.2
  54.8 9.5 all-gather.1
  80.9 13.1 reduce-scatter.4
where the time goes:
time: 136 us
  blocking collectives  63.6 us (47%)
  waiting for transfers between devices  31.4 us (23%)
  matrix products  23.2 us (17%)
  between operations  13.2 us (10%)
  other arithmetic  3.48 us (3%)
    all_to_all x1, blocking collectives, on_device(): lax.all_to_all(outgoing, 'expert', split_axis=0, concat_axis=0, tiled=True)  31.9 us
    all_to_all x1, blocking collectives, on_device(): lax.all_to_all(results, 'expert', split_axis=0, concat_axis=0, tiled=True)  31.8 us
    reduce_scatter x1, waiting for transfers between devices, on_device(): lax.psum_scatter(partial_value, 'tensor', scatter_dimension=2, tiled=True)  13.4 us
    dot_general x1, matrix products, on_device(): jnp.einsum('snh,hl->snl', hidden, w_down, preferred_element_type=jnp.floa...  10.5 us
    all_gather x1, waiting for transfers between devices, on_device(): lax.all_gather(lax.all_to_all(outgoing, 'expert', split_axis=0, concat_ax...  9.71 us
    reduce_scatter x1, waiting for transfers between devices, on_device(): lax.psum_scatter(partial_latent, 'tensor', scatter_dimension=1, tiled=True)  8.23 us
    dot_general x1, matrix products, on_device(): jnp.einsum('snl,lh->snh', slot_rows, w_gate, preferred_element_type=jnp.f...  5.89 us
    dot_general x1, matrix products, on_device(): jnp.dot(tokens, latent_down, preferred_element_type=jnp.float32)  4 us
  transfers between devices with their start and end apart: 3, of which 3 were waited for; matrix products, arithmetic and copies ran while one was open for 2% of the time, Pallas kernels for 0%

commit v1 on v0

--- a/solution.py
+++ b/solution.py
@@ -1,7 +1,15 @@
+import functools
+
 import jax
 import jax.numpy as jnp
 from jax import lax
+from jax.experimental import pallas as pl
+from jax.experimental.pallas import tpu as pltpu
 from jax.sharding import PartitionSpec as P
+
+MESH = pl.DeviceIdType.MESH
+F32 = jnp.float32
+BF16 = jnp.bfloat16
 
 
 def slot_tables(route_rows, gate_rows, devices, capacity):
@@ -20,15 +28,12 @@
     return (placing, mixing)
 
 
-def on_device(tokens, latent_down, expert_gate, expert_up, expert_down, routes, gates):
+def by_slots(tokens, latent_down, expert_gate, expert_up, expert_down, routes, gates):
     devices = lax.axis_size("expert")
     row_count, per_row = routes.shape
     capacity = 2 * row_count * per_row // devices
     placing, mixing = slot_tables(routes, gates, devices, capacity)
     partial_latent = jnp.dot(tokens, latent_down, preferred_element_type=jnp.float32)
-    w_gate = expert_gate[0]
-    w_up = expert_up[0]
-    w_down = expert_down[0]
     latent = lax.psum_scatter(partial_latent, "tensor", scatter_dimension=1, tiled=True).astype(
         jnp.bfloat16
     )
@@ -40,10 +45,14 @@
         axis=2,
         tiled=True,
     )
-    gate_part = jnp.einsum("snl,lh->snh", slot_rows, w_gate, preferred_element_type=jnp.float32)
-    up_part = jnp.einsum("snl,lh->snh", slot_rows, w_up, preferred_element_type=jnp.float32)
+    gate_part = jnp.einsum(
+        "snl,lh->snh", slot_rows, expert_gate[0], preferred_element_type=jnp.float32
+    )
+    up_part = jnp.einsum("snl,lh->snh", slot_rows, expert_up[0], preferred_element_type=jnp.float32)
     hidden = (jax.nn.silu(gate_part) * up_part).astype(jnp.bfloat16)
-    partial_value = jnp.einsum("snh,hl->snl", hidden, w_down, preferred_element_type=jnp.float32)
+    partial_value = jnp.einsum(
+        "snh,hl->snl", hidden, expert_down[0], preferred_element_type=jnp.float32
+    )
     results = lax.psum_scatter(partial_value, "tensor", scatter_dimension=2, tiled=True).astype(
         jnp.bfloat16
     )
@@ -53,6 +62,343 @@
         mixing, returned_rows, precision=lax.Precision.HIGHEST, preferred_element_type=jnp.float32
     )
     return mixed.astype(jnp.bfloat16)
+
+
+def tile_of(size):
+    return 256 if size % 256 == 0 else 128
+
+
+def kernel(
+    lines,
+    tokens_hbm,
+    down_hbm,
+    wg_hbm,
+    wu_hbm,
+    wd_hbm,
+    routes_ref,
+    gates_ref,
+    out_ref,
+    tok,
+    ld,
+    wg,
+    wu,
+    wd,
+    lat_out,
+    lat_in,
+    lat_own,
+    table,
+    x,
+    hid,
+    p_out,
+    p_in,
+    own,
+    keep,
+    y_out,
+    y_in,
+    z_out,
+    z_in,
+    load_sem,
+    lat_sem,
+    gt_send,
+    gt_recv,
+    az_send,
+    az_recv,
+    ay_send,
+    ay_recv,
+    ac_send,
+    ac_recv,
+    pc_send,
+    pc_recv,
+    ry_send,
+    ry_recv,
+    rz_send,
+    rz_recv,
+):
+    e = lax.axis_index("expert")
+    t = lax.axis_index("tensor")
+    n = 2 * lines
+    z, y = e // 2, lax.rem(e, 2)
+    rows = tok.shape[0]
+    half = out_ref.shape[1]
+    other_y = 1 - y
+    mate = {"tensor": 1 - t}
+    beside = {"expert": z * 2 + other_y}
+
+    def at(shift):
+        return lax.rem(e + shift, n)
+
+    barrier = pltpu.get_barrier_semaphore()
+    for shift in range(1, n):
+        pl.semaphore_signal(barrier, inc=1, device_id={"expert": at(shift)}, device_id_type=MESH)
+    pl.semaphore_signal(barrier, inc=1, device_id=mate, device_id_type=MESH)
+
+    mate_cols = pl.ds(pl.multiple_of((1 - t) * half, half), half)
+    own_cols = pl.ds(pl.multiple_of(t * half, half), half)
+    loads = [
+        pltpu.make_async_copy(tokens_hbm, tok, load_sem.at[0]),
+        pltpu.make_async_copy(down_hbm.at[:, mate_cols], ld.at[0], load_sem.at[1]),
+        pltpu.make_async_copy(down_hbm.at[:, own_cols], ld.at[1], load_sem.at[2]),
+        pltpu.make_async_copy(wg_hbm.at[0], wg, load_sem.at[3]),
+        pltpu.make_async_copy(wu_hbm.at[0], wu, load_sem.at[4]),
+        pltpu.make_async_copy(wd_hbm.at[0], wd, load_sem.at[5]),
+    ]
+    for load in loads[:3]:
+        load.start()
+
+    experts = lax.broadcasted_iota(jnp.int32, (n, rows), 0)
+    weight = jnp.zeros((n, rows), F32)
+    for k in range(routes_ref.shape[0]):
+        weight += jnp.where(routes_ref[k : k + 1, :] == experts, gates_ref[k : k + 1, :], 0.0)
+    table[e] = weight
+
+    loads[0].wait()
+    loads[1].wait()
+    for load in loads[3:]:
+        load.start()
+
+    lat_out[...] = jnp.dot(tok[...], ld[0], preferred_element_type=F32)
+    pl.semaphore_wait(barrier, n)
+
+    def remote(src, dst, send, recv, where):
+        return pltpu.make_async_remote_copy(
+            src_ref=src,
+            dst_ref=dst,
+            send_sem=send,
+            recv_sem=recv,
+            device_id=where,
+            device_id_type=MESH,
+        )
+
+    lat_copy = remote(lat_out, lat_in, lat_sem.at[0], lat_sem.at[1], mate)
+    lat_copy.start()
+    tables = []
+    for shift in range(1, n):
+        copy = remote(
+            table.at[e], table.at[e], gt_send.at[shift], gt_recv.at[shift], {"expert": at(shift)}
+        )
+        copy.start()
+        tables.append(copy)
+    loads[2].wait()
+    lat_own[...] = jnp.dot(tok[...], ld[1], preferred_element_type=F32)
+
+    def block(index):
+        return pl.ds(pl.multiple_of(index * rows, rows), rows)
+
+    def line(step):
+        return lax.rem(z + lines - step, lines)
+
+    def piece(step, side):
+        return x.at[t, block(line(step) * 2 + side)]
+
+    az = [None] * lines
+    ay = [None] * lines
+    ac = [[None, None] for _ in range(lines)]
+    for step in range(lines):
+        mine = x.at[t, block(e)]
+        if step:
+            target = {"expert": lax.rem(z + step, lines) * 2 + y}
+            az[step] = remote(mine, mine, az_send.at[step], az_recv.at[step], target)
+        source = piece(step, y)
+        ay[step] = remote(source, source, ay_send.at[step], ay_recv.at[step], beside)
+        for place, side in enumerate((y, other_y)):
+            source = piece(step, side)
+            ac[step][place] = remote(
+                source, source, ac_send.at[step, place], ac_recv.at[step, place], mate
+            )
+
+    lat_copy.wait_recv()
+    x[t, block(e)] = (lat_own[...] + lat_in[...]).astype(BF16)
+    ay[0].start()
+    for step in range(1, lines):
+        az[step].start()
+    ac[0][0].start()
+
+    def pass_on(step):
+        az[step].wait_recv()
+        ay[step].start()
+        ac[step][0].start()
+
+    def pass_over(step):
+        ay[step].wait_recv()
+        ac[step][1].start()
+
+    hidden_units = wg.shape[1]
+
+    def up(step):
+        for place in range(2):
+            ac[step][place].wait_recv()
+        pair = pl.ds(pl.multiple_of(line(step) * 2 * rows, 2 * rows), 2 * rows)
+        width = tile_of(hidden_units)
+
+        @pl.loop(0, hidden_units // width)
+        def _(j):
+            cols = pl.ds(pl.multiple_of(j * width, width), width)
+            item = jnp.concatenate([x[0, pair], x[1, pair]], axis=1)
+            g = jnp.dot(item, wg[:, cols], preferred_element_type=F32)
+            u = jnp.dot(item, wu[:, cols], preferred_element_type=F32)
+            hid[:, cols] = (g / (1.0 + jnp.exp(-g)) * u).astype(BF16)
+
+    pc = [
+        remote(p_out.at[s], p_in.at[s], pc_send.at[s], pc_recv.at[s], mate) for s in range(lines)
+    ]
+    ry = [
+        remote(y_out.at[s], y_in.at[s], ry_send.at[s], ry_recv.at[s], beside) for s in range(lines)
+    ]
+    rz = [None] + [
+        remote(
+            z_out.at[s], z_in.at[s], rz_send.at[s], rz_recv.at[s], {"expert": line(s) * 2 + y}
+        )
+        for s in range(1, lines)
+    ]
+
+    def down(step):
+        width = tile_of(half)
+
+        @pl.loop(0, half // width)
+        def _(j):
+            cols = pl.ds(pl.multiple_of((1 - t) * half + j * width, width), width)
+            here = pl.ds(pl.multiple_of(j * width, width), width)
+            p_out[step, :, here] = jnp.dot(
+                hid[...], wd[:, cols], preferred_element_type=F32
+            ).astype(BF16)
+
+        pc[step].start()
+
+        @pl.loop(0, half // width)
+        def _(j):
+            cols = pl.ds(pl.multiple_of(t * half + j * width, width), width)
+            here = pl.ds(pl.multiple_of(j * width, width), width)
+            own[step, :, here] = jnp.dot(hid[...], wd[:, cols], preferred_element_type=F32)
+
+    diagonal = lax.broadcasted_iota(jnp.int32, (rows, rows), 0) == lax.broadcasted_iota(
+        jnp.int32, (rows, rows), 1
+    )
+
+    def scaled(step, side):
+        part = block(side)
+        across = table[line(step) * 2 + side, pl.ds(e, 1), :]
+        column = jnp.sum(jnp.where(diagonal, across, 0.0), axis=1, keepdims=True)
+        return (own[step, part] + p_in[step, part].astype(F32)) * column
+
+    def back_over(step):
+        pc[step].wait_recv()
+        y_out[step] = scaled(step, other_y).astype(BF16)
+        ry[step].start()
+        keep[step] = scaled(step, y)
+
+    def back_home(step):
+        ry[step].wait_recv()
+        total = keep[step] + y_in[step].astype(F32)
+        if step == 0:
+            keep[0] = total
+        else:
+            z_out[step] = total.astype(BF16)
+            rz[step].start()
+
+    order = list(range(1, lines))
+    pass_over(0)
+    loads[3].wait()
+    loads[4].wait()
+    pass_on(order[0])
+    up(0)
+    for later in order[1:]:
+        pass_on(later)
+    loads[5].wait()
+    down(0)
+    for copy in tables:
+        copy.wait_recv()
+    steps = [0] + order
+    for place in range(1, lines):
+        pass_over(steps[place])
+        up(steps[place])
+        back_over(steps[place - 1])
+        down(steps[place])
+        back_home(steps[place - 1])
+    back_over(steps[-1])
+    back_home(steps[-1])
+
+    total = keep[0]
+    for step in order:
+        rz[step].wait_recv()
+        total += z_in[step].astype(F32)
+    out_ref[...] = total.astype(BF16)
+
+    lat_copy.wait_send()
+    for copy in tables + az[1:] + ay + [c for pair in ac for c in pair] + pc + ry + rz[1:]:
+        copy.wait_send()
+
+
+def by_rows(tokens, latent_down, expert_gate, expert_up, expert_down, routes, gates):
+    n = lax.axis_size("expert")
+    lines = n // 2
+    rows, features = tokens.shape
+    width = latent_down.shape[1]
+    half = width // 2
+    units = expert_gate.shape[2]
+    vmem = pl.BlockSpec(memory_space=pltpu.VMEM)
+    hbm = pl.BlockSpec(memory_space=pl.ANY)
+    dma = pltpu.SemaphoreType.DMA
+    flops = 2 * rows * features * width + 6 * n * rows * width * units
+    return pl.pallas_call(
+        functools.partial(kernel, lines),
+        out_shape=jax.ShapeDtypeStruct((rows, half), BF16),
+        in_specs=[hbm] * 5 + [vmem] * 2,
+        out_specs=vmem,
+        scratch_shapes=[
+            pltpu.VMEM((rows, features), BF16),
+            pltpu.VMEM((2, features, half), BF16),
+            pltpu.VMEM((width, units), BF16),
+            pltpu.VMEM((width, units), BF16),
+            pltpu.VMEM((units, width), BF16),
+            pltpu.VMEM((rows, half), F32),
+            pltpu.VMEM((rows, half), F32),
+            pltpu.VMEM((rows, half), F32),
+            pltpu.VMEM((n, n, rows), F32),
+            pltpu.VMEM((2, n * rows, half), BF16),
+            pltpu.VMEM((2 * rows, units), BF16),
+            pltpu.VMEM((lines, 2 * rows, half), BF16),
+            pltpu.VMEM((lines, 2 * rows, half), BF16),
+            pltpu.VMEM((lines, 2 * rows, half), F32),
+            pltpu.VMEM((lines, rows, half), F32),
+            pltpu.VMEM((lines, rows, half), BF16),
+            pltpu.VMEM((lines, rows, half), BF16),
+            pltpu.VMEM((lines, rows, half), BF16),
+            pltpu.VMEM((lines, rows, half), BF16),
+            dma((6,)),
+            dma((2,)),
+            dma((n,)),
+            dma((n,)),
+            dma((lines,)),
+            dma((lines,)),
+            dma((lines,)),
+            dma((lines,)),
+            dma((lines, 2)),
+            dma((lines, 2)),
+            dma((lines,)),
+            dma((lines,)),
+            dma((lines,)),
+            dma((lines,)),
+            dma((lines,)),
+            dma((lines,)),
+        ],
+        compiler_params=pltpu.CompilerParams(
+            collective_id=0, has_side_effects=True, vmem_limit_bytes=48 * 1024 * 1024
+        ),
+        cost_estimate=pl.CostEstimate(
+            flops=flops,
+            bytes_accessed=2 * (rows * features + features * width + 3 * width * units),
+            transcendentals=n * rows * units,
+        ),
+        name="latent_experts",
+    )(tokens, latent_down, expert_gate, expert_up, expert_down, routes.T, gates.T)
+
+
+def on_device(tokens, latent_down, expert_gate, expert_up, expert_down, routes, gates):
+    devices = lax.axis_size("expert")
+    rows, per_row = routes.shape
+    capacity = 2 * rows * per_row // devices
+    form = by_rows if capacity >= rows and devices % 2 == 0 else by_slots
+    return form(tokens, latent_down, expert_gate, expert_up, expert_down, routes, gates)
 
 
 def solution(mesh):

time: 136 us -> 63.2 us (0.46)
  blocking collectives: 63.6 us -> 0 us
  Pallas kernels: 0 us -> 56.7 us
  waiting for transfers between devices: 31.4 us -> 0 us
  matrix products: 23.2 us -> 0 us
  between operations: 13.2 us -> 0.01 us
  local copies, waits for them, and re-layouts: 0.73 us -> 6.24 us
  other arithmetic: 3.48 us -> 0 us
    all_to_all x2 -> x0, blocking collectives: 63.6 us -> none  [the longest x1 31.9 us: on_device(): lax.all_to_all(outgoing, 'expert', split_axis=0, concat_axis=0, tiled=True)]
    pallas_call x0 -> x1, Pallas kernels: none -> 56.7 us  [by_rows(): pl.pallas_call(functools.partial(kernel, lines), out_shape=jax.ShapeDtype...]
    dot_general x5 -> x0, matrix products: 23.2 us -> none  [the longest x1 10.5 us: on_device(): jnp.einsum('snh,hl->snl', hidden, w_down, preferred_element_type=jnp.floa...]
    reduce_scatter x2 -> x0, waiting for transfers between devices: 21.6 us -> none  [the longest x1 13.4 us: on_device(): lax.psum_scatter(partial_value, 'tensor', scatter_dimension=2, tiled=True)]
    all_gather x1 -> x0, waiting for transfers between devices: 9.71 us -> none  [on_device(): lax.all_gather(lax.all_to_all(outgoing, 'expert', split_axis=0, concat_ax...]
    unnamed x7 -> x11, local copies, waits for them, and re-layouts: 0.12 us -> 6.24 us
    convert_element_type x2 -> x0, other arithmetic: 1.73 us -> none  [the longest x1 1.72 us: on_device(): lax.psum_scatter(partial_value, 'tensor', scatter_dimension=2, tiled=True)]
  transfers between devices with their start and end apart: 3 -> 0, of which waited for: 3 -> 0; matrix products, arithmetic and copies ran while one was open for 2% -> 0% of each run, Pallas kernels for 0% -> 0%
where the time goes in v1:
time: 63.2 us; the launch traced here: 62.9 us
  Pallas kernels  56.7 us (90%)
  local copies, waits for them, and re-layouts  6.24 us (10%)
    pallas_call x1, Pallas kernels, by_rows(): pl.pallas_call(functools.partial(kernel, lines), out_shape=jax.ShapeDtype...  56.7 us
    unnamed x11, local copies, waits for them, and re-layouts  6.24 us

profile of v1, /device:TPU:0, one launch (start us, length us, event | category | flops | bytes accessed | tf_op | source)
XLA Modules:
  0.0 62.9 jit_solution(4333022177983616242)
XLA Ops:
  0.0 0.0 copy-start
  0.0 1.6 %copy-done = bf16[1,1024,1024]{2,1,0:T(8,128)(2,1)S(1)} copy-done((bf16[1,1024,1024]{2,1,0:T(8,128)(2,1)S(1)}, bf16[1,1024,1024]{2,1,0:T(8,128)(2,1)}, u32[]{:S(2)}) %copy-start) | copy-done | bytes 2097176
  1.6 0.0 copy-start.1
  1.6 1.6 %copy-done.1 = bf16[1,1024,1024]{2,1,0:T(8,128)(2,1)S(1)} copy-done((bf16[1,1024,1024]{2,1,0:T(8,128)(2,1)S(1)}, bf16[1,1024,1024]{2,1,0:T(8,128)(2,1)}, u32[]{:S(2)}) %copy-start.1) | copy-done | bytes 2097176
  3.2 0.0 copy-start.2
  3.2 1.0 %copy-done.2 = bf16[128,2048]{1,0:T(8,128)(2,1)S(1)} copy-done((bf16[128,2048]{1,0:T(8,128)(2,1)S(1)}, bf16[128,2048]{1,0:T(8,128)(2,1)}, u32[]{:S(2)}) %copy-start.2) | copy-done | bytes 524312
  4.2 0.0 copy-start.3
  4.2 0.7 %copy-done.3 = s32[128,4]{0,1:T(4,128)S(1)} copy-done((s32[128,4]{0,1:T(4,128)S(1)}, s32[128,4]{0,1:T(4,128)}, u32[]{:S(2)}) %copy-start.3) | copy-done | bytes 2072
  4.9 0.0 copy-start.4
  4.9 0.7 %copy-done.4 = f32[128,4]{0,1:T(4,128)S(1)} copy-done((f32[128,4]{0,1:T(4,128)S(1)}, f32[128,4]{0,1:T(4,128)}, u32[]{:S(2)}) %copy-start.4) | copy-done | bytes 2072
  5.6 56.7 %latent_experts.1 = bf16[128,512]{1,0:T(8,128)(2,1)S(1)} custom-call(bf16[128,2048]{1,0:T(8,128)(2,1)S(1)} %copy-done.2, bf16[2048,1024]{1,0:T(8,128)(2,1)} %down_hbm.1, bf16[1,1024,1024]{2,1,0:T(8,128)(2,1)S(1)} %copy-done, bf16[1,1024,1024]{2,1,0:T(8,128)(2,1)S(1)} %copy-done.1, bf16[1,1024,1024]{2,1,0:T(8,128)(2,1)} %wd_hbm.1, s32[4,128]{1,0:T(4,128)S(1)} %bitcast.2, ...), custom_call_target="tpu_custom_call" | custom-call | flops 6979321856 | bytes 11010048 | tf_op jit(solution)/shard_map/latent_experts/pallas_call | solution.py:342
  62.2 0.7 %copy.9 = bf16[128,512]{1,0:T(8,128)(2,1)} copy(bf16[128,512]{1,0:T(8,128)(2,1)S(1)} %latent_experts.1) | data formatting | bytes 262144
Async XLA Ops:
  0.0 1.6 %copy-start = (bf16[1,1024,1024]{2,1,0:T(8,128)(2,1)S(1)}, bf16[1,1024,1024]{2,1,0:T(8,128)(2,1)}, u32[]{:S(2)}) copy-start(bf16[1,1024,1024]{2,1,0:T(8,128)(2,1)} %wg_hbm.1) | copy-start | bytes 6291460
  1.6 1.6 %copy-start.1 = (bf16[1,1024,1024]{2,1,0:T(8,128)(2,1)S(1)}, bf16[1,1024,1024]{2,1,0:T(8,128)(2,1)}, u32[]{:S(2)}) copy-start(bf16[1,1024,1024]{2,1,0:T(8,128)(2,1)} %wu_hbm.1) | copy-start | bytes 6291460
  3.2 1.0 %copy-start.2 = (bf16[128,2048]{1,0:T(8,128)(2,1)S(1)}, bf16[128,2048]{1,0:T(8,128)(2,1)}, u32[]{:S(2)}) copy-start(bf16[128,2048]{1,0:T(8,128)(2,1)} %tokens_hbm.1) | copy-start | bytes 1572868
  4.2 0.7 %copy-start.3 = (s32[128,4]{0,1:T(4,128)S(1)}, s32[128,4]{0,1:T(4,128)}, u32[]{:S(2)}) copy-start(s32[128,4]{0,1:T(4,128)} %param.12) | copy-start | bytes 6148
  4.9 0.7 %copy-start.4 = (f32[128,4]{0,1:T(4,128)S(1)}, f32[128,4]{0,1:T(4,128)}, u32[]{:S(2)}) copy-start(f32[128,4]{0,1:T(4,128)} %param.13) | copy-start | bytes 6148

commit v2 on v1

--- a/solution.py
+++ b/solution.py
@@ -75,9 +75,11 @@
     wg_hbm,
     wu_hbm,
     wd_hbm,
+    routes_hbm,
+    gates_hbm,
+    out_ref,
     routes_ref,
     gates_ref,
-    out_ref,
     tok,
     ld,
     wg,
@@ -99,8 +101,10 @@
     z_in,
     load_sem,
     lat_sem,
-    gt_send,
-    gt_recv,
+    tz_send,
+    tz_recv,
+    ty_send,
+    ty_recv,
     az_send,
     az_recv,
     ay_send,
@@ -124,13 +128,13 @@
     mate = {"tensor": 1 - t}
     beside = {"expert": z * 2 + other_y}
 
-    def at(shift):
-        return lax.rem(e + shift, n)
-
+    def along(step):
+        return {"expert": lax.rem(z + step, lines) * 2 + y}
+
+    partners = [along(step) for step in range(1, lines)] + [beside, mate]
     barrier = pltpu.get_barrier_semaphore()
-    for shift in range(1, n):
-        pl.semaphore_signal(barrier, inc=1, device_id={"expert": at(shift)}, device_id_type=MESH)
-    pl.semaphore_signal(barrier, inc=1, device_id=mate, device_id_type=MESH)
+    for partner in partners:
+        pl.semaphore_signal(barrier, inc=1, device_id=partner, device_id_type=MESH)
 
     mate_cols = pl.ds(pl.multiple_of((1 - t) * half, half), half)
     own_cols = pl.ds(pl.multiple_of(t * half, half), half)
@@ -141,9 +145,13 @@
         pltpu.make_async_copy(wg_hbm.at[0], wg, load_sem.at[3]),
         pltpu.make_async_copy(wu_hbm.at[0], wu, load_sem.at[4]),
         pltpu.make_async_copy(wd_hbm.at[0], wd, load_sem.at[5]),
+        pltpu.make_async_copy(routes_hbm, routes_ref, load_sem.at[6]),
+        pltpu.make_async_copy(gates_hbm, gates_ref, load_sem.at[7]),
     ]
-    for load in loads[:3]:
+    for load in loads[6:] + loads[:3]:
         load.start()
+    loads[6].wait()
+    loads[7].wait()
 
     experts = lax.broadcasted_iota(jnp.int32, (n, rows), 0)
     weight = jnp.zeros((n, rows), F32)
@@ -153,11 +161,11 @@
 
     loads[0].wait()
     loads[1].wait()
-    for load in loads[3:]:
+    for load in loads[3:6]:
         load.start()
 
     lat_out[...] = jnp.dot(tok[...], ld[0], preferred_element_type=F32)
-    pl.semaphore_wait(barrier, n)
+    pl.semaphore_wait(barrier, len(partners))
 
     def remote(src, dst, send, recv, where):
         return pltpu.make_async_remote_copy(
@@ -171,13 +179,6 @@
 
     lat_copy = remote(lat_out, lat_in, lat_sem.at[0], lat_sem.at[1], mate)
     lat_copy.start()
-    tables = []
-    for shift in range(1, n):
-        copy = remote(
-            table.at[e], table.at[e], gt_send.at[shift], gt_recv.at[shift], {"expert": at(shift)}
-        )
-        copy.start()
-        tables.append(copy)
     loads[2].wait()
     lat_own[...] = jnp.dot(tok[...], ld[1], preferred_element_type=F32)
 
@@ -190,14 +191,20 @@
     def piece(step, side):
         return x.at[t, block(line(step) * 2 + side)]
 
+    tz = [None] * lines
+    ty = [None] * lines
     az = [None] * lines
     ay = [None] * lines
     ac = [[None, None] for _ in range(lines)]
     for step in range(lines):
         mine = x.at[t, block(e)]
         if step:
-            target = {"expert": lax.rem(z + step, lines) * 2 + y}
-            az[step] = remote(mine, mine, az_send.at[step], az_recv.at[step], target)
+            az[step] = remote(mine, mine, az_send.at[step], az_recv.at[step], along(step))
+            tz[step] = remote(
+                table.at[e], table.at[e], tz_send.at[step], tz_recv.at[step], along(step)
+            )
+        passed = table.at[line(step) * 2 + y]
+        ty[step] = remote(passed, passed, ty_send.at[step], ty_recv.at[step], beside)
         source = piece(step, y)
         ay[step] = remote(source, source, ay_send.at[step], ay_recv.at[step], beside)
         for place, side in enumerate((y, other_y)):
@@ -208,19 +215,26 @@
 
     lat_copy.wait_recv()
     x[t, block(e)] = (lat_own[...] + lat_in[...]).astype(BF16)
+    order = list(range(1, lines))
     ay[0].start()
-    for step in range(1, lines):
+    ac[0][0].start()
+    for step in order:
         az[step].start()
-    ac[0][0].start()
+    ty[0].start()
+    for step in order:
+        tz[step].start()
 
     def pass_on(step):
         az[step].wait_recv()
         ay[step].start()
         ac[step][0].start()
+        tz[step].wait_recv()
+        ty[step].start()
 
     def pass_over(step):
         ay[step].wait_recv()
         ac[step][1].start()
+        ty[step].wait_recv()
 
     hidden_units = wg.shape[1]
 
@@ -230,7 +244,7 @@
         pair = pl.ds(pl.multiple_of(line(step) * 2 * rows, 2 * rows), 2 * rows)
         width = tile_of(hidden_units)
 
-        @pl.loop(0, hidden_units // width)
+        @pl.loop(0, hidden_units // width, unroll=True)
         def _(j):
             cols = pl.ds(pl.multiple_of(j * width, width), width)
             item = jnp.concatenate([x[0, pair], x[1, pair]], axis=1)
@@ -254,7 +268,7 @@
     def down(step):
         width = tile_of(half)
 
-        @pl.loop(0, half // width)
+        @pl.loop(0, half // width, unroll=True)
         def _(j):
             cols = pl.ds(pl.multiple_of((1 - t) * half + j * width, width), width)
             here = pl.ds(pl.multiple_of(j * width, width), width)
@@ -264,7 +278,7 @@
 
         pc[step].start()
 
-        @pl.loop(0, half // width)
+        @pl.loop(0, half // width, unroll=True)
         def _(j):
             cols = pl.ds(pl.multiple_of(t * half + j * width, width), width)
             here = pl.ds(pl.multiple_of(j * width, width), width)
@@ -295,25 +309,27 @@
             z_out[step] = total.astype(BF16)
             rz[step].start()
 
-    order = list(range(1, lines))
+    steps = [0] + order
     pass_over(0)
+    pass_on(order[0])
     loads[3].wait()
     loads[4].wait()
-    pass_on(order[0])
     up(0)
-    for later in order[1:]:
-        pass_on(later)
+    for step in order[1:2]:
+        pass_on(step)
     loads[5].wait()
     down(0)
-    for copy in tables:
-        copy.wait_recv()
-    steps = [0] + order
     for place in range(1, lines):
         pass_over(steps[place])
+        if place + 2 < lines:
+            pass_on(steps[place + 2])
+        if place > 1:
+            back_home(steps[place - 2])
+        back_over(steps[place - 1])
         up(steps[place])
-        back_over(steps[place - 1])
         down(steps[place])
-        back_home(steps[place - 1])
+    if lines > 1:
+        back_home(steps[-2])
     back_over(steps[-1])
     back_home(steps[-1])
 
@@ -324,7 +340,7 @@
     out_ref[...] = total.astype(BF16)
 
     lat_copy.wait_send()
-    for copy in tables + az[1:] + ay + [c for pair in ac for c in pair] + pc + ry + rz[1:]:
+    for copy in tz[1:] + ty + az[1:] + ay + [c for pair in ac for c in pair] + pc + ry + rz[1:]:
         copy.wait_send()
 
 
@@ -336,15 +352,17 @@
     half = width // 2
     units = expert_gate.shape[2]
     vmem = pl.BlockSpec(memory_space=pltpu.VMEM)
-    hbm = pl.BlockSpec(memory_space=pl.ANY)
+    hbm = pl.BlockSpec(memory_space=pltpu.HBM)
     dma = pltpu.SemaphoreType.DMA
     flops = 2 * rows * features * width + 6 * n * rows * width * units
     return pl.pallas_call(
         functools.partial(kernel, lines),
         out_shape=jax.ShapeDtypeStruct((rows, half), BF16),
-        in_specs=[hbm] * 5 + [vmem] * 2,
+        in_specs=[hbm] * 7,
         out_specs=vmem,
         scratch_shapes=[
+            pltpu.VMEM(routes.shape[::-1], jnp.int32),
+            pltpu.VMEM(gates.shape[::-1], F32),
             pltpu.VMEM((rows, features), BF16),
             pltpu.VMEM((2, features, half), BF16),
             pltpu.VMEM((width, units), BF16),
@@ -364,10 +382,12 @@
             pltpu.VMEM((lines, rows, half), BF16),
             pltpu.VMEM((lines, rows, half), BF16),
             pltpu.VMEM((lines, rows, half), BF16),
-            dma((6,)),
+            dma((8,)),
             dma((2,)),
-            dma((n,)),
-            dma((n,)),
+            dma((lines,)),
+            dma((lines,)),
+            dma((lines,)),
+            dma((lines,)),
             dma((lines,)),
             dma((lines,)),
             dma((lines,)),

time: 63.2 us -> 56.3 us (0.89)
  Pallas kernels: 56.7 us -> 49.8 us
    pallas_call x1, Pallas kernels: 56.7 us -> 49.8 us  [by_rows(): pl.pallas_call(functools.partial(kernel, lines), out_shape=jax.ShapeDtype...]
where the time goes in v2:
time: 56.3 us; the launch traced here: 56.1 us
  Pallas kernels  49.8 us (88%)
  local copies, waits for them, and re-layouts  6.24 us (11%)
    pallas_call x1, Pallas kernels, by_rows(): pl.pallas_call(functools.partial(kernel, lines), out_shape=jax.ShapeDtype...  49.8 us
    unnamed x11, local copies, waits for them, and re-layouts  6.24 us

profile of v2, /device:TPU:0, one launch (start us, length us, event | category | flops | bytes accessed | tf_op | source)
XLA Modules:
  0.0 56.1 jit_solution(4054736468061481075)
XLA Ops:
  0.0 0.0 copy-start
  0.0 1.6 %copy-done = bf16[1,1024,1024]{2,1,0:T(8,128)(2,1)S(1)} copy-done((bf16[1,1024,1024]{2,1,0:T(8,128)(2,1)S(1)}, bf16[1,1024,1024]{2,1,0:T(8,128)(2,1)}, u32[]{:S(2)}) %copy-start) | copy-done | bytes 2097176
  1.6 0.0 copy-start.1
  1.6 1.6 %copy-done.1 = bf16[1,1024,1024]{2,1,0:T(8,128)(2,1)S(1)} copy-done((bf16[1,1024,1024]{2,1,0:T(8,128)(2,1)S(1)}, bf16[1,1024,1024]{2,1,0:T(8,128)(2,1)}, u32[]{:S(2)}) %copy-start.1) | copy-done | bytes 2097176
  3.2 0.0 copy-start.2
  3.2 1.0 %copy-done.2 = bf16[128,2048]{1,0:T(8,128)(2,1)S(1)} copy-done((bf16[128,2048]{1,0:T(8,128)(2,1)S(1)}, bf16[128,2048]{1,0:T(8,128)(2,1)}, u32[]{:S(2)}) %copy-start.2) | copy-done | bytes 524312
  4.2 0.0 copy-start.3
  4.2 0.7 %copy-done.3 = s32[128,4]{0,1:T(4,128)S(1)} copy-done((s32[128,4]{0,1:T(4,128)S(1)}, s32[128,4]{0,1:T(4,128)}, u32[]{:S(2)}) %copy-start.3) | copy-done | bytes 2072
  4.9 0.0 copy-start.4
  4.9 0.7 %copy-done.4 = f32[128,4]{0,1:T(4,128)S(1)} copy-done((f32[128,4]{0,1:T(4,128)S(1)}, f32[128,4]{0,1:T(4,128)}, u32[]{:S(2)}) %copy-start.4) | copy-done | bytes 2072
  5.6 49.8 %latent_experts.1 = bf16[128,512]{1,0:T(8,128)(2,1)S(1)} custom-call(bf16[128,2048]{1,0:T(8,128)(2,1)S(1)} %copy-done.2, bf16[2048,1024]{1,0:T(8,128)(2,1)} %down_hbm.1, bf16[1,1024,1024]{2,1,0:T(8,128)(2,1)S(1)} %copy-done, bf16[1,1024,1024]{2,1,0:T(8,128)(2,1)S(1)} %copy-done.1, bf16[1,1024,1024]{2,1,0:T(8,128)(2,1)} %wd_hbm.1, s32[4,128]{1,0:T(4,128)S(1)} %bitcast.2, ...), custom_call_target="tpu_custom_call" | custom-call | flops 6979321856 | bytes 11010048 | tf_op jit(solution)/shard_map/latent_experts/pallas_call | solution.py:358
  55.4 0.7 %copy.9 = bf16[128,512]{1,0:T(8,128)(2,1)} copy(bf16[128,512]{1,0:T(8,128)(2,1)S(1)} %latent_experts.1) | data formatting | bytes 262144
Async XLA Ops:
  0.0 1.6 %copy-start = (bf16[1,1024,1024]{2,1,0:T(8,128)(2,1)S(1)}, bf16[1,1024,1024]{2,1,0:T(8,128)(2,1)}, u32[]{:S(2)}) copy-start(bf16[1,1024,1024]{2,1,0:T(8,128)(2,1)} %wg_hbm.1) | copy-start | bytes 6291460
  1.6 1.6 %copy-start.1 = (bf16[1,1024,1024]{2,1,0:T(8,128)(2,1)S(1)}, bf16[1,1024,1024]{2,1,0:T(8,128)(2,1)}, u32[]{:S(2)}) copy-start(bf16[1,1024,1024]{2,1,0:T(8,128)(2,1)} %wu_hbm.1) | copy-start | bytes 6291460
  3.2 1.0 %copy-start.2 = (bf16[128,2048]{1,0:T(8,128)(2,1)S(1)}, bf16[128,2048]{1,0:T(8,128)(2,1)}, u32[]{:S(2)}) copy-start(bf16[128,2048]{1,0:T(8,128)(2,1)} %tokens_hbm.1) | copy-start | bytes 1572868
  4.2 0.7 %copy-start.3 = (s32[128,4]{0,1:T(4,128)S(1)}, s32[128,4]{0,1:T(4,128)}, u32[]{:S(2)}) copy-start(s32[128,4]{0,1:T(4,128)} %param.12) | copy-start | bytes 6148
  4.9 0.7 %copy-start.4 = (f32[128,4]{0,1:T(4,128)S(1)}, f32[128,4]{0,1:T(4,128)}, u32[]{:S(2)}) copy-start(f32[128,4]{0,1:T(4,128)} %param.13) | copy-start | bytes 6148

commit v3 on v2

--- a/solution.py
+++ b/solution.py
@@ -165,6 +165,8 @@
         load.start()
 
     lat_out[...] = jnp.dot(tok[...], ld[0], preferred_element_type=F32)
+    loads[2].wait()
+    lat_own[...] = jnp.dot(tok[...], ld[1], preferred_element_type=F32)
     pl.semaphore_wait(barrier, len(partners))
 
     def remote(src, dst, send, recv, where):
@@ -179,8 +181,6 @@
 
     lat_copy = remote(lat_out, lat_in, lat_sem.at[0], lat_sem.at[1], mate)
     lat_copy.start()
-    loads[2].wait()
-    lat_own[...] = jnp.dot(tok[...], ld[1], preferred_element_type=F32)
 
     def block(index):
         return pl.ds(pl.multiple_of(index * rows, rows), rows)
@@ -213,6 +213,9 @@
                 source, source, ac_send.at[step, place], ac_recv.at[step, place], mate
             )
 
+    ty[0].start()
+    for step in range(1, lines):
+        tz[step].start()
     lat_copy.wait_recv()
     x[t, block(e)] = (lat_own[...] + lat_in[...]).astype(BF16)
     order = list(range(1, lines))
@@ -220,9 +223,6 @@
     ac[0][0].start()
     for step in order:
         az[step].start()
-    ty[0].start()
-    for step in order:
-        tz[step].start()
 
     def pass_on(step):
         az[step].wait_recv()

time: 56.3 us -> 55.7 us (0.989)
  Pallas kernels: 49.8 us -> 49.2 us
    pallas_call x1, Pallas kernels: 49.8 us -> 49.2 us  [by_rows(): pl.pallas_call(functools.partial(kernel, lines), out_shape=jax.ShapeDtype...]
where the time goes in v3:
time: 55.7 us; the launch traced here: 55.4 us
  Pallas kernels  49.2 us (88%)
  local copies, waits for them, and re-layouts  6.24 us (11%)
    pallas_call x1, Pallas kernels, by_rows(): pl.pallas_call(functools.partial(kernel, lines), out_shape=jax.ShapeDtype...  49.2 us
    unnamed x11, local copies, waits for them, and re-layouts  6.24 us

profile of v3, /device:TPU:0, one launch (start us, length us, event | category | flops | bytes accessed | tf_op | source)
XLA Modules:
  0.0 55.4 jit_solution(62869256772368080)
XLA Ops:
  0.0 0.0 copy-start
  0.0 1.6 %copy-done = bf16[1,1024,1024]{2,1,0:T(8,128)(2,1)S(1)} copy-done((bf16[1,1024,1024]{2,1,0:T(8,128)(2,1)S(1)}, bf16[1,1024,1024]{2,1,0:T(8,128)(2,1)}, u32[]{:S(2)}) %copy-start) | copy-done | bytes 2097176
  1.6 0.0 copy-start.1
  1.6 1.6 %copy-done.1 = bf16[1,1024,1024]{2,1,0:T(8,128)(2,1)S(1)} copy-done((bf16[1,1024,1024]{2,1,0:T(8,128)(2,1)S(1)}, bf16[1,1024,1024]{2,1,0:T(8,128)(2,1)}, u32[]{:S(2)}) %copy-start.1) | copy-done | bytes 2097176
  3.2 0.0 copy-start.2
  3.2 1.0 %copy-done.2 = bf16[128,2048]{1,0:T(8,128)(2,1)S(1)} copy-done((bf16[128,2048]{1,0:T(8,128)(2,1)S(1)}, bf16[128,2048]{1,0:T(8,128)(2,1)}, u32[]{:S(2)}) %copy-start.2) | copy-done | bytes 524312
  4.2 0.0 copy-start.3
  4.2 0.7 %copy-done.3 = s32[128,4]{0,1:T(4,128)S(1)} copy-done((s32[128,4]{0,1:T(4,128)S(1)}, s32[128,4]{0,1:T(4,128)}, u32[]{:S(2)}) %copy-start.3) | copy-done | bytes 2072
  4.9 0.0 copy-start.4
  4.9 0.7 %copy-done.4 = f32[128,4]{0,1:T(4,128)S(1)} copy-done((f32[128,4]{0,1:T(4,128)S(1)}, f32[128,4]{0,1:T(4,128)}, u32[]{:S(2)}) %copy-start.4) | copy-done | bytes 2072
  5.6 49.2 %latent_experts.1 = bf16[128,512]{1,0:T(8,128)(2,1)S(1)} custom-call(bf16[128,2048]{1,0:T(8,128)(2,1)S(1)} %copy-done.2, bf16[2048,1024]{1,0:T(8,128)(2,1)} %down_hbm.1, bf16[1,1024,1024]{2,1,0:T(8,128)(2,1)S(1)} %copy-done, bf16[1,1024,1024]{2,1,0:T(8,128)(2,1)S(1)} %copy-done.1, bf16[1,1024,1024]{2,1,0:T(8,128)(2,1)} %wd_hbm.1, s32[4,128]{1,0:T(4,128)S(1)} %bitcast.2, ...), custom_call_target="tpu_custom_call" | custom-call | flops 6979321856 | bytes 11010048 | tf_op jit(solution)/shard_map/latent_experts/pallas_call | solution.py:358
  54.8 0.7 %copy.9 = bf16[128,512]{1,0:T(8,128)(2,1)} copy(bf16[128,512]{1,0:T(8,128)(2,1)S(1)} %latent_experts.1) | data formatting | bytes 262144
Async XLA Ops:
  0.0 1.6 %copy-start = (bf16[1,1024,1024]{2,1,0:T(8,128)(2,1)S(1)}, bf16[1,1024,1024]{2,1,0:T(8,128)(2,1)}, u32[]{:S(2)}) copy-start(bf16[1,1024,1024]{2,1,0:T(8,128)(2,1)} %wg_hbm.1) | copy-start | bytes 6291460
  1.6 1.6 %copy-start.1 = (bf16[1,1024,1024]{2,1,0:T(8,128)(2,1)S(1)}, bf16[1,1024,1024]{2,1,0:T(8,128)(2,1)}, u32[]{:S(2)}) copy-start(bf16[1,1024,1024]{2,1,0:T(8,128)(2,1)} %wu_hbm.1) | copy-start | bytes 6291460
  3.2 1.0 %copy-start.2 = (bf16[128,2048]{1,0:T(8,128)(2,1)S(1)}, bf16[128,2048]{1,0:T(8,128)(2,1)}, u32[]{:S(2)}) copy-start(bf16[128,2048]{1,0:T(8,128)(2,1)} %tokens_hbm.1) | copy-start | bytes 1572868
  4.2 0.7 %copy-start.3 = (s32[128,4]{0,1:T(4,128)S(1)}, s32[128,4]{0,1:T(4,128)}, u32[]{:S(2)}) copy-start(s32[128,4]{0,1:T(4,128)} %param.12) | copy-start | bytes 6148
  4.9 0.7 %copy-start.4 = (f32[128,4]{0,1:T(4,128)S(1)}, f32[128,4]{0,1:T(4,128)}, u32[]{:S(2)}) copy-start(f32[128,4]{0,1:T(4,128)} %param.13) | copy-start | bytes 6148
